TPU v7x, 32 devices: a whole 2x2x4 slice. The times are simulated.
32 devices in a mesh: grid: 16 (over z, x, core), mem: 2 (over y).
Axes of the slice: x: 2, y: 2, z: 4, core: 2. Of those that a mesh axis runs over, the one named last changes fastest.
Arguments:
- ens: bfloat16 [20, 4, 32, 16384], P('mem', None, None, 'grid'), may hold values from -6 to 6
- control: float32 [4, 32, 16384], P(None, None, 'grid'), may hold values from -6 to 6
- col_count: int32 [128], P('grid'), may hold values from 64 to 128, as said below
- level_index: int32 [32], replicated, may hold values from 43 to 136, as said below
- pair_blocks: int32 [1536, 2], P('grid'), may hold values from 0 to 127, as said below
- loc_blocks: bfloat16 [1536, 128, 128], P('grid'), may hold values from -0.109375 to 0.109375
Outputs:
- mixed: float32 [4, 32, 16384], P(None, None, ('grid', 'mem'))
Inputs may be any that keep to these rules, and one draw needn't show every extreme that they name: `pair_blocks`: rows come in groups of 12, one group for each block b in order; group b holds the pairs (b, (b + k) mod 128) for k = 0, k = 12 and 10 further distinct k between 1 and 11. `col_count`: some block is full. `level_index`: strictly increasing by steps of 1 to 3; the last is 136.
All inputs are finite; a program needn't handle non-finite values.
Results may differ from a plain program's by a relative error of at most 0.0029.
Values may be sent and summed in bfloat16 or wider, within the bound.
A program may use at most 64 MiB of HBM per device.

v0:
```python
import jax
import jax.numpy as jnp
from jax import lax
from jax.sharding import PartitionSpec as P

SPAN = 12


vertical_scale = 8.0


def passed_along(array, axis, by):
    peers = lax.axis_size(axis)
    return lax.ppermute(array, axis, [(i, (i + by) % peers) for i in range(peers)])


def per_device(ens, control, col_count, level_index, pair_blocks, loc_blocks):
    blocks_dev = col_count.shape[0]
    width = loc_blocks.shape[1]
    per_block = pair_blocks.shape[0] // blocks_dev
    reach = (blocks_dev - 1 + SPAN) // blocks_dev
    devices = lax.axis_size("grid")
    here = lax.axis_index("grid")
    members_dev = ens.shape[0]
    slot_count = ens.shape[1]
    level_count = ens.shape[2]
    columns = jnp.arange(blocks_dev * width)
    live = (columns % width < jnp.repeat(col_count, width)).astype(jnp.float32)
    masked = control * live
    levels = level_index.astype(jnp.float32)
    vert = jnp.exp(-jnp.abs(levels[:, None] - levels[None, :]) / vertical_scale)
    weighted = jnp.sum(ens.astype(jnp.float32) * masked[None], axis=1)
    lifted = jnp.einsum("kl,mlc->mkc", vert, weighted, precision=lax.Precision.HIGHEST).astype(
        jnp.bfloat16
    )
    own = lifted.reshape(members_dev, level_count, blocks_dev, width).transpose(2, 0, 1, 3)
    ens_blocks = ens.reshape(members_dev, slot_count, level_count, blocks_dev, width)
    fetched = [own]
    for offset in range(1, reach + 1):
        fetched.append(passed_along(own, "grid", -offset))
    table = jnp.concatenate(fetched, axis=0)
    far_count = (reach + 1) * blocks_dev
    first = pair_blocks[:, 0]
    second = pair_blocks[:, 1]
    near_index = first - here * blocks_dev
    distance = jnp.mod(second // blocks_dev - here, devices)
    far_index = distance * blocks_dev + second % blocks_dev

    def pair_group(carry, item):
        near_acc, far_acc = carry
        group_id, near_idx, far_idx, local_loc = item
        near_rows = own[group_id]
        far_rows = table[far_idx]
        to_near = jnp.einsum(
            "pab,pmlb->mla", local_loc, far_rows, preferred_element_type=jnp.float32
        )
        apart = (far_idx != near_idx).astype(jnp.float32)
        to_far = jnp.einsum(
            "pab,mla->pmlb", local_loc, near_rows, preferred_element_type=jnp.float32
        )
        to_far = to_far * apart[:, None, None, None]
        near_acc = near_acc.at[group_id].add(to_near)
        far_acc = far_acc.at[far_idx].add(to_far)
        return ((near_acc, far_acc), None)

    near_start = jnp.zeros((blocks_dev, members_dev, level_count, width), jnp.float32)
    far_start = jnp.zeros((far_count, members_dev, level_count, width), jnp.float32)
    items = (
        jnp.arange(blocks_dev, dtype=jnp.int32),
        near_index.reshape(blocks_dev, per_block),
        far_index.reshape(blocks_dev, per_block),
        loc_blocks.reshape(blocks_dev, per_block, width, width),
    )
    (near_acc, far_acc), unused = lax.scan(pair_group, (near_start, far_start), items)
    far_parts = far_acc.reshape(reach + 1, blocks_dev, members_dev, level_count, width)
    spread = near_acc + far_parts[0]
    for offset in range(1, reach + 1):
        spread = spread + passed_along(far_parts[offset], "grid", offset)
    summed = jnp.sum(ens_blocks.astype(jnp.float32) * spread.transpose(1, 2, 0, 3)[:, None], axis=0)
    members_all = members_dev * lax.axis_size("mem")
    terms = summed.reshape(slot_count, level_count, blocks_dev * width) * live / (members_all - 1)
    return lax.psum_scatter(terms, "mem", scatter_dimension=2, tiled=True)


def solution(mesh):
    return jax.shard_map(
        per_device,
        mesh=mesh,
        in_specs=(
            P("mem", None, None, "grid"),
            P(None, None, "grid"),
            P("grid"),
            P(),
            P("grid", None),
            P("grid", None, None),
        ),
        out_specs=P(None, None, ("grid", "mem")),
        check_vma=False,
    )
```

profile of v0, /device:TPU:26, one launch (start us, length us, event | category | flops | bytes accessed | tf_op | source)
XLA Modules:
  0.0 227.9 jit_solution(17086207633109151868)
XLA Ops:
  9.0 2.5 %fusion.13 = f32[10,32,1024]{2,1,0:T(8,128)S(1)} fusion(bf16[10,4,32,1024]{3,2,1,0:T(8,128)(2,1)} %param.10, f32[4,32,1024]{2,1,0:T(8,128)S(1)} %broadcast_multiply_fusion), kind=kLoop, calls=%fused_computation.25 | loop fusion | flops 3604480 | bytes 4456448 | tf_op jit(solution)/shard_map/reduce_sum | solution.py:32
  15.1 18.1 %collective-permute-done.1 = bf16[8,10,32,128]{3,2,1,0:T(8,128)(2,1)S(1)} collective-permute-done((bf16[8,10,32,128]{3,2,1,0:T(8,128)(2,1)}, bf16[8,10,32,128]{3,2,1,0:T(8,128)(2,1)S(1)}, u32[]{:S(2)}, u32[]{:S(2)}) %collective-permute-start.1) | collective-permute-done | bytes 655392 | tf_op jit(solution)/shard_map/ppermute | solution.py:14
  33.2 2.5 %collective-permute-done = bf16[8,10,32,128]{3,2,1,0:T(8,128)(2,1)S(1)} collective-permute-done((bf16[8,10,32,128]{3,2,1,0:T(8,128)(2,1)}, bf16[8,10,32,128]{3,2,1,0:T(8,128)(2,1)S(1)}, u32[]{:S(2)}, u32[]{:S(2)}) %collective-permute-start) | collective-permute-done | bytes 655392 | tf_op jit(solution)/shard_map/ppermute | solution.py:14
  35.7 2.6 %pad_maximum_fusion = bf16[24,10,32,128]{3,2,1,0:T(8,128)(2,1)} fusion(bf16[8,10,32,128]{3,2,1,0:T(8,128)(2,1)S(1)} %collective-permute-done.1, bf16[8,10,32,128]{3,2,1,0:T(8,128)(2,1)S(1)} %collective-permute-done, bf16[8,10,32,128]{3,2,1,0:T(8,128)(2,1)} %bitcast.57), kind=kLoop, calls=%fused_computation.27 | loop fusion | flops 1966080 | bytes 3932160 | tf_op jit(solution)/shard_map/concatenate | solution.py:41
  38.5 2.4 %broadcast_in_dim.7 = f32[24,10,32,128]{3,2,1,0:T(8,128)} broadcast(f32[]{:T(128)} %constant.97.clone.1), dimensions={} | broadcast | bytes 3932164 | tf_op jit(solution)/shard_map/broadcast_in_dim | solution.py:67
  40.8 111.5 %while.13 = (s32[]{:T(128)}, f32[8,10,32,128]{3,2,1,0:T(8,128)S(1)}, f32[24,10,32,128]{3,2,1,0:T(8,128)}, s32[8]{0:T(128)S(1)}, s32[8,12]{1,0:T(8,128)S(1)}, /*i...) while((s32[]{:T(128)}, ...), condition=%wide.region_4.5_spmd, body=%wide.region_1.4_spmd.sunk | while | flops 252724320 | bytes 15947924 | solution.py:74
  44.1 2.3 %gather_fusion = bf16[12,10,32,128]{3,2,1,0:T(8,128)(2,1)S(1)} fusion(bf16[24,10,32,128]{3,2,1,0:T(8,128)(2,1)} %get-tuple-element.177, s32[1024]{0:T(1024)S(1)} %pad_clamp_fusion.2), kind=kCustom, calls=%fused_computation.clone.1 | custom fusion | bytes 1966128 | tf_op jit(solution)/shard_map/while/body/eval_jaxpr/gather | solution.py:53
  50.1 4.7 %scatter_fusion = f32[24,10,32,128]{3,2,1,0:T(8,128)} fusion(f32[24,10,32,128]{3,2,1,0:T(8,128)} %get-tuple-element.160, s32[12]{0:T(128)S(1)} %fusion.50, f32[12,10,32,128]{3,2,1,0:T(8,128)S(1)} %copy.23), kind=kCustom, calls=%fused_computation.1.clone.1 | custom fusion | flops 491520 | bytes 5898288 | tf_op jit(solution)/shard_map/while/body/eval_jaxpr/scatter-add | solution.py:63
  58.1 2.3 %gather_fusion = bf16[12,10,32,128]{3,2,1,0:T(8,128)(2,1)S(1)} fusion(bf16[24,10,32,128]{3,2,1,0:T(8,128)(2,1)} %get-tuple-element.177, s32[1024]{0:T(1024)S(1)} %pad_clamp_fusion.2), kind=kCustom, calls=%fused_computation.clone.1 | custom fusion | bytes 1966128 | tf_op jit(solution)/shard_map/while/body/eval_jaxpr/gather | solution.py:53
  64.1 4.6 %scatter_fusion = f32[24,10,32,128]{3,2,1,0:T(8,128)} fusion(f32[24,10,32,128]{3,2,1,0:T(8,128)} %get-tuple-element.160, s32[12]{0:T(128)S(1)} %fusion.50, f32[12,10,32,128]{3,2,1,0:T(8,128)S(1)} %copy.23), kind=kCustom, calls=%fused_computation.1.clone.1 | custom fusion | flops 491520 | bytes 5898288 | tf_op jit(solution)/shard_map/while/body/eval_jaxpr/scatter-add | solution.py:63
  72.0 2.3 %gather_fusion = bf16[12,10,32,128]{3,2,1,0:T(8,128)(2,1)S(1)} fusion(bf16[24,10,32,128]{3,2,1,0:T(8,128)(2,1)} %get-tuple-element.177, s32[1024]{0:T(1024)S(1)} %pad_clamp_fusion.2), kind=kCustom, calls=%fused_computation.clone.1 | custom fusion | bytes 1966128 | tf_op jit(solution)/shard_map/while/body/eval_jaxpr/gather | solution.py:53
  78.0 4.7 %scatter_fusion = f32[24,10,32,128]{3,2,1,0:T(8,128)} fusion(f32[24,10,32,128]{3,2,1,0:T(8,128)} %get-tuple-element.160, s32[12]{0:T(128)S(1)} %fusion.50, f32[12,10,32,128]{3,2,1,0:T(8,128)S(1)} %copy.23), kind=kCustom, calls=%fused_computation.1.clone.1 | custom fusion | flops 491520 | bytes 5898288 | tf_op jit(solution)/shard_map/while/body/eval_jaxpr/scatter-add | solution.py:63
  85.9 2.3 %gather_fusion = bf16[12,10,32,128]{3,2,1,0:T(8,128)(2,1)S(1)} fusion(bf16[24,10,32,128]{3,2,1,0:T(8,128)(2,1)} %get-tuple-element.177, s32[1024]{0:T(1024)S(1)} %pad_clamp_fusion.2), kind=kCustom, calls=%fused_computation.clone.1 | custom fusion | bytes 1966128 | tf_op jit(solution)/shard_map/while/body/eval_jaxpr/gather | solution.py:53
  91.9 4.7 %scatter_fusion = f32[24,10,32,128]{3,2,1,0:T(8,128)} fusion(f32[24,10,32,128]{3,2,1,0:T(8,128)} %get-tuple-element.160, s32[12]{0:T(128)S(1)} %fusion.50, f32[12,10,32,128]{3,2,1,0:T(8,128)S(1)} %copy.23), kind=kCustom, calls=%fused_computation.1.clone.1 | custom fusion | flops 491520 | bytes 5898288 | tf_op jit(solution)/shard_map/while/body/eval_jaxpr/scatter-add | solution.py:63
  99.9 2.3 %gather_fusion = bf16[12,10,32,128]{3,2,1,0:T(8,128)(2,1)S(1)} fusion(bf16[24,10,32,128]{3,2,1,0:T(8,128)(2,1)} %get-tuple-element.177, s32[1024]{0:T(1024)S(1)} %pad_clamp_fusion.2), kind=kCustom, calls=%fused_computation.clone.1 | custom fusion | bytes 1966128 | tf_op jit(solution)/shard_map/while/body/eval_jaxpr/gather | solution.py:53
  105.9 4.7 %scatter_fusion = f32[24,10,32,128]{3,2,1,0:T(8,128)} fusion(f32[24,10,32,128]{3,2,1,0:T(8,128)} %get-tuple-element.160, s32[12]{0:T(128)S(1)} %fusion.50, f32[12,10,32,128]{3,2,1,0:T(8,128)S(1)} %copy.23), kind=kCustom, calls=%fused_computation.1.clone.1 | custom fusion | flops 491520 | bytes 5898288 | tf_op jit(solution)/shard_map/while/body/eval_jaxpr/scatter-add | solution.py:63
  119.8 4.6 %scatter_fusion = f32[24,10,32,128]{3,2,1,0:T(8,128)} fusion(f32[24,10,32,128]{3,2,1,0:T(8,128)} %get-tuple-element.160, s32[12]{0:T(128)S(1)} %fusion.50, f32[12,10,32,128]{3,2,1,0:T(8,128)S(1)} %copy.23), kind=kCustom, calls=%fused_computation.1.clone.1 | custom fusion | flops 491520 | bytes 5898288 | tf_op jit(solution)/shard_map/while/body/eval_jaxpr/scatter-add | solution.py:63
  133.8 4.6 %scatter_fusion = f32[24,10,32,128]{3,2,1,0:T(8,128)} fusion(f32[24,10,32,128]{3,2,1,0:T(8,128)} %get-tuple-element.160, s32[12]{0:T(128)S(1)} %fusion.50, f32[12,10,32,128]{3,2,1,0:T(8,128)S(1)} %copy.23), kind=kCustom, calls=%fused_computation.1.clone.1 | custom fusion | flops 491520 | bytes 5898288 | tf_op jit(solution)/shard_map/while/body/eval_jaxpr/scatter-add | solution.py:63
  141.7 2.3 %gather_fusion = bf16[12,10,32,128]{3,2,1,0:T(8,128)(2,1)S(1)} fusion(bf16[24,10,32,128]{3,2,1,0:T(8,128)(2,1)} %get-tuple-element.177, s32[1024]{0:T(1024)S(1)} %pad_clamp_fusion.2), kind=kCustom, calls=%fused_computation.clone.1 | custom fusion | bytes 1966128 | tf_op jit(solution)/shard_map/while/body/eval_jaxpr/gather | solution.py:53
  147.7 4.6 %scatter_fusion = f32[24,10,32,128]{3,2,1,0:T(8,128)} fusion(f32[24,10,32,128]{3,2,1,0:T(8,128)} %get-tuple-element.160, s32[12]{0:T(128)S(1)} %fusion.50, f32[12,10,32,128]{3,2,1,0:T(8,128)S(1)} %copy.23), kind=kCustom, calls=%fused_computation.1.clone.1 | custom fusion | flops 491520 | bytes 5898288 | tf_op jit(solution)/shard_map/while/body/eval_jaxpr/scatter-add | solution.py:63
  154.3 4.4 %collective-permute-start.2 = (f32[8,10,32,128]{3,2,1,0:T(8,128)S(1)}, f32[8,10,32,128]{3,2,1,0:T(8,128)S(1)}, u32[]{:S(2)}, u32[]{:S(2)}) collective-permute-start(f32[8,10,32,128]{3,2,1,0:T(8,128)S(1)} %get-tuple-element.87), channel_id=1, source_target_pairs={{0,2},{2,4},{4,6},{6,8},{8,10},{10,12},{12,14},{14,16},{16,18},{18... | collective-permute-start | bytes 3932168 | tf_op jit(solution)/shard_map/ppermute | solution.py:14
  158.7 21.9 %collective-permute-done.2 = f32[8,10,32,128]{3,2,1,0:T(8,128)S(1)} collective-permute-done((f32[8,10,32,128]{3,2,1,0:T(8,128)S(1)}, f32[8,10,32,128]{3,2,1,0:T(8,128)S(1)}, u32[]{:S(2)}, u32[]{:S(2)}) %collective-permute-start.2) | collective-permute-done | bytes 1310752 | tf_op jit(solution)/shard_map/ppermute | solution.py:14
  180.6 9.8 %collective-permute-done.3 = f32[8,10,32,128]{3,2,1,0:T(8,128)S(1)} collective-permute-done((f32[8,10,32,128]{3,2,1,0:T(8,128)S(1)}, f32[8,10,32,128]{3,2,1,0:T(8,128)S(1)}, u32[]{:S(2)}, u32[]{:S(2)}) %collective-permute-start.3) | collective-permute-done | bytes 1310752 | tf_op jit(solution)/shard_map/ppermute | solution.py:14
  194.0 27.0 %reduce-scatter.2.cloned.1.call-done = f32[4,32,512]{2,1,0:T(8,128)} async-done(((f32[4,32,1024]{2,1,0:T(8,128)}), f32[4,32,512]{2,1,0:T(8,128)}) %reduce-scatter.2.cloned.1.call-update) | async-done | bytes 262160 | tf_op jit(solution)/shard_map/reduce_scatter | solution.py:82
  (92 shorter events, 57.2 us)
Async XLA Ops:
  6.5 214.5 %reduce-scatter.2.cloned.1.call-start = ((), (), s32[]{:S(2)}) async-start(), calls=%async_computation.1 | async-start | bytes 786432 | tf_op jit(solution)/shard_map/reduce_scatter | solution.py:82
  11.6 3.4 %copy-start.2 = (s32[96,2]{0,1:T(2,128)S(1)}, s32[96,2]{0,1:T(2,128)}, u32[]{:S(2)}) copy-start(s32[96,2]{0,1:T(2,128)} %param.14) | copy-start | bytes 2308
  13.8 19.4 %collective-permute-start.1 = (bf16[8,10,32,128]{3,2,1,0:T(8,128)(2,1)}, bf16[8,10,32,128]{3,2,1,0:T(8,128)(2,1)S(1)}, u32[]{:S(2)}, u32[]{:S(2)}) collective-permute-start(bf16[8,10,32,128]{3,2,1,0:T(8,128)(2,1)} %bitcast.57), channel_id=1, source_target_pairs={{0,28},{2,30},{4,0},{6,2},{8,4},{10,6},{12,8},{14,10},{16,12},{18,... | collective-permute-start | bytes 1966088 | tf_op jit(solution)/shard_map/ppermute | solution.py:14
  14.4 21.3 %collective-permute-start = (bf16[8,10,32,128]{3,2,1,0:T(8,128)(2,1)}, bf16[8,10,32,128]{3,2,1,0:T(8,128)(2,1)S(1)}, u32[]{:S(2)}, u32[]{:S(2)}) collective-permute-start(bf16[8,10,32,128]{3,2,1,0:T(8,128)(2,1)} %bitcast.57), channel_id=1, source_target_pairs={{0,30},{2,0},{4,2},{6,4},{8,6},{10,8},{12,10},{14,12},{16,14},{18,... | collective-permute-start | bytes 1966088 | tf_op jit(solution)/shard_map/ppermute | solution.py:14
  38.4 2.4 %copy-start.1 = (s32[4]{0:T(128)S(1)}, s32[4]{0:T(128)}, u32[]{:S(2)}) copy-start(s32[4]{0:T(128)} %constant.92.clone.1) | copy-start | bytes 52
  154.3 26.3 %collective-permute-start.2 = (f32[8,10,32,128]{3,2,1,0:T(8,128)S(1)}, f32[8,10,32,128]{3,2,1,0:T(8,128)S(1)}, u32[]{:S(2)}, u32[]{:S(2)}) collective-permute-start(f32[8,10,32,128]{3,2,1,0:T(8,128)S(1)} %get-tuple-element.87), channel_id=1, source_target_pairs={{0,2},{2,4},{4,6},{6,8},{8,10},{10,12},{12,14},{14,16},{16,18},{18... | collective-permute-start | bytes 3932168 | tf_op jit(solution)/shard_map/ppermute | solution.py:14
  158.7 31.7 %collective-permute-start.3 = (f32[8,10,32,128]{3,2,1,0:T(8,128)S(1)}, f32[8,10,32,128]{3,2,1,0:T(8,128)S(1)}, u32[]{:S(2)}, u32[]{:S(2)}) collective-permute-start(f32[8,10,32,128]{3,2,1,0:T(8,128)S(1)} %get-tuple-element.88), channel_id=1, source_target_pairs={{0,4},{2,6},{4,8},{6,10},{8,12},{10,14},{12,16},{14,18},{16,20},{1... | collective-permute-start | bytes 3932168 | tf_op jit(solution)/shard_map/ppermute | solution.py:14
  190.4 2.1 copy-start
Sparse Core Ops, SparseCore 0:
  194.2 26.8 reduce-scatter.1
where the time goes:
time: 231 us; the launch traced here: 228 us
  waiting for transfers between devices  79.3 us (34%)
  other arithmetic  54.4 us (24%)
  local copies, waits for them, and re-layouts  30.8 us (13%)
  matrix products  29.2 us (13%)
  loops' own time  15.2 us (7%)
  between operations  13.5 us (6%)
  starting transfers between devices  5.5 us (2%)
    ppermute x4, waiting for transfers between devices, passed_along(): lax.ppermute(array, axis, [(i, (i + by) % peers) for i in range(peers)])  52.3 us
    scatter-add x8, other arithmetic, pair_group(): far_acc = far_acc.at[far_idx].add(to_far)  37.1 us
    reduce_scatter x1, waiting for transfers between devices, per_device(): return lax.psum_scatter(terms, 'mem', scatter_dimension=2, tiled=True)  27 us
    gather x8, local copies, waits for them, and re-layouts, pair_group(): far_rows = table[far_idx]  18.2 us
    dot_general x8, matrix products, pair_group(): jnp.einsum('pab,pmlb->mla', local_loc, far_rows, preferred_element_type=j...  16.3 us
    another operation x1, loops' own time, per_device(): lax.scan(pair_group, (near_start, far_start), items)  15.2 us
    dot_general x8, matrix products, pair_group(): jnp.einsum('pab,mla->pmlb', local_loc, near_rows, preferred_element_type=...  11.6 us
    another operation x8, other arithmetic  6.18 us
  transfers between devices with their start and end apart: 5, of which 5 were waited for; matrix products, arithmetic and copies ran while one was open for 0% of the time, Pallas kernels for 0%

commit v1 on v0

v1 whole, which is shorter than its diff:
```python
import functools

import jax
import jax.numpy as jnp
from jax import lax
from jax.experimental import pallas as pl
from jax.experimental.pallas import tpu as pltpu
from jax.sharding import PartitionSpec as P

SPAN = 12
MESH = pl.DeviceIdType.MESH


vertical_scale = 8.0


def kernel(
    sizes,
    count_ref,
    level_ref,
    slot_ref,
    ens_hbm,
    control_hbm,
    loc_hbm,
    out_ref,
    ens,
    control,
    loc,
    table,
    far,
    relay_in,
    near_in,
    spread,
    terms,
    terms_in,
    in_sems,
    lift_send,
    lift_recv,
    far_send,
    far_recv,
    term_send,
    term_recv,
):
    members, slots, levels, own, width, devices, peers = sizes
    rows = members * levels
    extra = SPAN - own
    pairs = loc_hbm.shape[0]
    here = lax.axis_index("grid")
    mem = lax.axis_index("mem")
    up = lax.rem(here + 1, devices)
    down = lax.rem(here + devices - 1, devices)

    def cols(first, last):
        return slice(first * width, last * width)

    step = 2 if own % 2 == 0 else 1
    parts = own // step
    loads = []
    for part in range(parts):
        at = cols(part * step, (part + 1) * step)
        a = pltpu.make_async_copy(
            control_hbm.at[:, :, at], control.at[:, :, at], in_sems.at[2 * part]
        )
        b = pltpu.make_async_copy(
            ens_hbm.at[:, :, :, at], ens.at[:, :, :, at], in_sems.at[2 * part + 1]
        )
        a.start()
        b.start()
        loads.append((a, b))
    load_loc = pltpu.make_async_copy(loc_hbm, loc.at[pl.ds(0, pairs)], in_sems.at[2 * parts])
    load_loc.start()

    barrier = pltpu.get_barrier_semaphore()
    for other in (up, down):
        pl.semaphore_signal(barrier, inc=1, device_id={"grid": other}, device_id_type=MESH)
    for away in range(1, peers):
        pl.semaphore_signal(
            barrier, inc=1, device_id={"mem": lax.rem(mem + away, peers)}, device_id_type=MESH
        )

    loc[pairs] = jnp.zeros((width, width), loc.dtype)

    group = max(g for g in range(1, members + 1) if members % g == 0 and g * levels <= 256)
    size = group * levels
    down_at = lax.broadcasted_iota(jnp.int32, (size, 1), 0)
    across_at = lax.broadcasted_iota(jnp.int32, (1, size), 1)
    level_down = jnp.zeros((size, 1), jnp.float32)
    level_across = jnp.zeros((1, size), jnp.float32)
    for l in range(levels):
        value = level_ref[l].astype(jnp.float32)
        level_down = jnp.where(down_at % levels == l, value, level_down)
        level_across = jnp.where(across_at % levels == l, value, level_across)
    vert = jnp.exp(-jnp.abs(level_down - level_across) / vertical_scale)
    vert = jnp.where(down_at // levels == across_at // levels, vert, 0.0)

    lane = lax.broadcasted_iota(jnp.int32, (1, width), 1)

    def live(block):
        return (lane < count_ref[block]).astype(jnp.float32)

    def lift_copy(which, src, dst, n):
        return pltpu.make_async_remote_copy(
            src_ref=table.at[:, cols(src, src + n)],
            dst_ref=table.at[:, cols(dst, dst + n)],
            send_sem=lift_send.at[which],
            recv_sem=lift_recv.at[which],
            device_id={"grid": down},
            device_id_type=MESH,
        )

    lift_copies = [
        lift_copy(0, 0, own, extra),
        lift_copy(1, extra, own + extra, own - extra),
        lift_copy(2, own, 2 * own, extra),
    ]

    def far_copy(which, src, dst_ref, n):
        return pltpu.make_async_remote_copy(
            src_ref=far.at[:, cols(src, src + n)],
            dst_ref=dst_ref,
            send_sem=far_send.at[which],
            recv_sem=far_recv.at[which],
            device_id={"grid": up},
            device_id_type=MESH,
        )

    far_copies = [
        far_copy(0, own, relay_in, extra),
        far_copy(1, extra, near_in.at[:, cols(extra, own)], own - extra),
        far_copy(2, 0, near_in.at[:, cols(0, extra)], extra),
    ]

    greeted = False
    for part in range(parts):
        loads[part][0].wait()
        loads[part][1].wait()
        at = cols(part * step, (part + 1) * step)
        mask = jnp.concatenate([live(part * step + s) for s in range(step)], axis=1)
        masked = [control[t, :, at] * mask for t in range(slots)]
        for g in range(members // group):
            weighted = []
            for m in range(g * group, (g + 1) * group):
                total = ens[m, 0, :, at].astype(jnp.float32) * masked[0]
                for t in range(1, slots):
                    total = total + ens[m, t, :, at].astype(jnp.float32) * masked[t]
                weighted.append(total)
            lifted = jnp.dot(
                vert,
                jnp.concatenate(weighted, axis=0),
                precision=lax.Precision.HIGHEST,
                preferred_element_type=jnp.float32,
            )
            table[g * size : (g + 1) * size, at] = lifted.astype(table.dtype)
        if not greeted:
            pl.semaphore_wait(barrier, 2 + peers - 1)
            greeted = True
        if part * step < extra <= (part + 1) * step:
            lift_copies[0].start()
    lift_copies[1].start()
    load_loc.wait()

    def pair(i, k):
        return loc[slot_ref[i * (SPAN + 1) + k]]

    def from_below(j, first, last):
        stack = jnp.concatenate([pair(i, j - i) for i in range(first, last)], axis=0)
        return jnp.dot(table[:, cols(first, last)], stack, preferred_element_type=jnp.float32)

    def from_above(j, first, last):
        stack = jnp.concatenate([pair(j, s - j) for s in range(first, last)], axis=1)
        return lax.dot_general(
            table[:, cols(first, last)],
            stack,
            (((1,), (1,)), ((), ())),
            preferred_element_type=jnp.float32,
        )

    for j in range(2 * own, own + SPAN):
        far[:, cols(j - own, j - own + 1)] = from_below(j, j - SPAN, own).astype(far.dtype)
    far_copies[0].start()
    for j in range(own + extra, 2 * own):
        far[:, cols(j - own, j - own + 1)] = from_below(j, j - SPAN, own).astype(far.dtype)
    far_copies[1].start()

    lift_copies[0].wait_recv()
    lift_copies[2].start()

    far_copies[0].wait_recv()
    for j in range(own, own + extra):
        first = max(0, j - SPAN)
        total = from_below(j, first, own) + relay_in[:, cols(j - own, j - own + 1)].astype(
            jnp.float32
        )
        far[:, cols(j - own, j - own + 1)] = total.astype(far.dtype)
    far_copies[2].start()

    for j in range(own):
        total = from_above(j, j, own)
        if j > 0:
            total = total + from_below(j, 0, j)
        spread[:, cols(j, j + 1)] = total

    lift_copies[1].wait_recv()
    for j in range(own):
        last = min(2 * own, j + SPAN + 1)
        spread[:, cols(j, j + 1)] += from_above(j, own, last)

    chunk = own // peers

    def finish(j):
        column = cols(j, j + 1)
        total = spread[:, column] + near_in[:, column].astype(jnp.float32)
        if j + SPAN >= 2 * own:
            total = total + from_above(j, 2 * own, j + SPAN + 1)
        scale = live(j) / (members * peers - 1)
        within = cols(j % chunk, j % chunk + 1)
        for t in range(slots):
            mixed = ens[0, t, :, column].astype(jnp.float32) * total[:levels]
            for m in range(1, members):
                mixed = mixed + ens[m, t, :, column].astype(jnp.float32) * (
                    total[m * levels : (m + 1) * levels]
                )
            terms[j // chunk, t, :, within] = mixed * scale

    def term_copy(to):
        return pltpu.make_async_remote_copy(
            src_ref=terms.at[to],
            dst_ref=terms_in.at[mem],
            send_sem=term_send.at[to],
            recv_sem=term_recv.at[mem],
            device_id={"mem": jnp.int32(to)},
            device_id_type=MESH,
        )

    far_copies[1].wait_recv()
    lift_copies[2].wait_recv()
    arrived = False
    for to in reversed(range(peers)):
        if to * chunk < extra and not arrived:
            far_copies[2].wait_recv()
            arrived = True
        for j in range(to * chunk, (to + 1) * chunk):
            finish(j)

        @pl.when(mem != to)
        def _():
            term_copy(to).start()

        @pl.when(mem == to)
        def _():
            terms_in[to] = terms[to]

    for source in range(peers):

        @pl.when(mem != source)
        def _():
            pltpu.make_async_remote_copy(
                src_ref=terms.at[source],
                dst_ref=terms_in.at[source],
                send_sem=term_send.at[source],
                recv_sem=term_recv.at[source],
                device_id={"mem": jnp.int32(source)},
                device_id_type=MESH,
            ).wait()

    result = terms_in[0]
    for source in range(1, peers):
        result = result + terms_in[source]
    out_ref[...] = result
    for copy in lift_copies + far_copies:
        copy.wait_send()


def per_device(ens, control, col_count, level_index, pair_blocks, loc_blocks):
    own = col_count.shape[0]
    width = loc_blocks.shape[1]
    pairs = pair_blocks.shape[0]
    per_block = pairs // own
    devices = lax.axis_size("grid")
    peers = lax.axis_size("mem")
    members, slots, levels, columns = ens.shape
    rows = members * levels
    assert own < SPAN <= 2 * own and own % peers == 0 and devices > 2
    extra = SPAN - own

    offsets = jnp.mod(pair_blocks[:, 1] - pair_blocks[:, 0], own * devices)
    offsets = offsets.reshape(own, 1, per_block)
    wanted = jnp.arange(SPAN + 1, dtype=jnp.int32).reshape(1, SPAN + 1, 1)
    place = jnp.arange(pairs, dtype=jnp.int32).reshape(own, 1, per_block)
    slot = jnp.min(jnp.where(offsets == wanted, place, pairs), axis=2).reshape(-1)

    smem = pl.BlockSpec(memory_space=pltpu.SMEM)
    anywhere = pl.BlockSpec(memory_space=pl.ANY)
    parts = own // 2 if own % 2 == 0 else own
    sizes = (members, slots, levels, own, width, devices, peers)
    share = columns // peers
    return pl.pallas_call(
        functools.partial(kernel, sizes),
        out_shape=jax.ShapeDtypeStruct((slots, levels, share), jnp.float32),
        in_specs=[smem, smem, smem, anywhere, anywhere, anywhere],
        out_specs=pl.BlockSpec(memory_space=pltpu.VMEM),
        scratch_shapes=[
            pltpu.VMEM(ens.shape, ens.dtype),
            pltpu.VMEM(control.shape, control.dtype),
            pltpu.VMEM((pairs + 1, width, width), loc_blocks.dtype),
            pltpu.VMEM((rows, (own + SPAN) * width), jnp.bfloat16),
            pltpu.VMEM((rows, SPAN * width), jnp.bfloat16),
            pltpu.VMEM((rows, extra * width), jnp.bfloat16),
            pltpu.VMEM((rows, columns), jnp.bfloat16),
            pltpu.VMEM((rows, columns), jnp.float32),
            pltpu.VMEM((peers, slots, levels, share), jnp.float32),
            pltpu.VMEM((peers, slots, levels, share), jnp.float32),
            pltpu.SemaphoreType.DMA((2 * parts + 1,)),
            pltpu.SemaphoreType.DMA((3,)),
            pltpu.SemaphoreType.DMA((3,)),
            pltpu.SemaphoreType.DMA((3,)),
            pltpu.SemaphoreType.DMA((3,)),
            pltpu.SemaphoreType.DMA((peers,)),
            pltpu.SemaphoreType.DMA((peers,)),
        ],
        compiler_params=pltpu.CompilerParams(
            collective_id=0, has_side_effects=True, vmem_limit_bytes=48 * 1024 * 1024
        ),
        cost_estimate=pl.CostEstimate(
            flops=2 * rows * width * width * pairs * 2,
            bytes_accessed=ens.size * 2 + control.size * 4 + loc_blocks.size * 2,
            transcendentals=0,
        ),
    )(col_count, level_index, slot, ens, control, loc_blocks)


def solution(mesh):
    return jax.shard_map(
        per_device,
        mesh=mesh,
        in_specs=(
            P("mem", None, None, "grid"),
            P(None, None, "grid"),
            P("grid"),
            P(),
            P("grid", None),
            P("grid", None, None),
        ),
        out_specs=P(None, None, ("grid", "mem")),
        check_vma=False,
    )
```

time: 231 us -> 39.9 us (0.17); the launches traced: 228 us -> 39.7 us
  waiting for transfers between devices: 79.3 us -> 0 us
  other arithmetic: 54.4 us -> 0.89 us
  Pallas kernels: 0 us -> 33.7 us
  matrix products: 29.2 us -> 0 us
  local copies, waits for them, and re-layouts: 30.8 us -> 5.04 us
  loops' own time: 15.2 us -> 0 us
  between operations: 13.5 us -> 0.02 us
  starting transfers between devices: 5.5 us -> 0 us
    ppermute x4 -> x0, waiting for transfers between devices: 52.3 us -> none  [passed_along(): lax.ppermute(array, axis, [(i, (i + by) % peers) for i in range(peers)])]
    scatter-add x8 -> x0, other arithmetic: 37.1 us -> none  [pair_group(): far_acc = far_acc.at[far_idx].add(to_far)]
    pallas_call x0 -> x1, Pallas kernels: none -> 33.7 us  [per_device(): pl.pallas_call(functools.partial(kernel, sizes), out_shape=jax.ShapeDtype...]
    dot_general x17 -> x0, matrix products: 29.2 us -> none  [the longest x8 16.3 us: pair_group(): jnp.einsum('pab,pmlb->mla', local_loc, far_rows, preferred_element_type=j...]
    reduce_scatter x1 -> x0, waiting for transfers between devices: 27 us -> none  [per_device(): return lax.psum_scatter(terms, 'mem', scatter_dimension=2, tiled=True)]
    gather x8 -> x0, local copies, waits for them, and re-layouts: 18.2 us -> none  [pair_group(): far_rows = table[far_idx]]
    another operation x1 -> x0, loops' own time: 15.2 us -> none  [per_device(): lax.scan(pair_group, (near_start, far_start), items)]
    another operation x8 -> x0, other arithmetic: 6.18 us -> none
  transfers between devices with their start and end apart: 5 -> 0, of which waited for: 5 -> 0; matrix products, arithmetic and copies ran while one was open for 0% -> 0% of each run, Pallas kernels for 0% -> 0%
where the time goes in v1:
time: 39.9 us; the launch traced here: 39.7 us
  Pallas kernels  33.7 us (84%)
  local copies, waits for them, and re-layouts  5.04 us (13%)
  other arithmetic  0.89 us (2%)
    pallas_call x1, Pallas kernels, per_device(): pl.pallas_call(functools.partial(kernel, sizes), out_shape=jax.ShapeDtype...  33.7 us
    unnamed x9, local copies, waits for them, and re-layouts  4.8 us

profile of v1, /device:TPU:26, one launch (start us, length us, event | category | flops | bytes accessed | tf_op | source)
XLA Modules:
  0.0 39.7 jit_solution(5257260788639683396)
XLA Ops:
  0.0 0.8 %subtract_reduce_fusion = s32[96]{0:T(128)S(1)} fusion(s32[96,2]{0,1:T(2,128)} %param.10), kind=kLoop, calls=%fused_computation.7 | loop fusion | flops 96 | bytes 1152 | tf_op jit(solution)/shard_map/sub | solution.py:286
  0.8 0.1 sub.11
  0.9 0.1 copy.7
  1.0 0.1 select_reduce_fusion
  1.1 0.1 reshape.49.slot_ref
  1.1 0.0 copy-start
  1.1 1.7 %copy-done = bf16[10,4,32,1024]{3,2,1,0:T(8,128)(2,1)S(1)} copy-done((bf16[10,4,32,1024]{3,2,1,0:T(8,128)(2,1)S(1)}, bf16[10,4,32,1024]{3,2,1,0:T(8,128)(2,1)}, u32[]{:S(2)}) %copy-start) | copy-done | bytes 2621464
  2.9 0.0 copy-start.1
  2.9 1.0 %copy-done.1 = f32[4,32,1024]{2,1,0:T(8,128)S(1)} copy-done((f32[4,32,1024]{2,1,0:T(8,128)S(1)}, f32[4,32,1024]{2,1,0:T(8,128)}, u32[]{:S(2)}) %copy-start.1) | copy-done | bytes 524312
  3.9 0.0 copy-start.2
  3.9 0.7 %copy-done.2 = s32[8]{0:T(128)S(1)} copy-done((s32[8]{0:T(128)S(1)}, s32[8]{0:T(128)}, u32[]{:S(2)}) %copy-start.2) | copy-done | bytes 56
  4.6 0.0 copy-start.3
  4.6 0.7 %copy-done.3 = s32[32]{0:T(128)S(1)} copy-done((s32[32]{0:T(128)S(1)}, s32[32]{0:T(128)}, u32[]{:S(2)}) %copy-start.3) | copy-done | bytes 152
  5.2 33.7 %shard_map.64 = f32[4,32,512]{2,1,0:T(8,128)S(1)} custom-call(s32[8]{0:T(128)S(1)} %copy-done.2, s32[32]{0:T(128)S(1)} %copy-done.3, s32[104]{0:T(128)S(1)} %reshape.49.slot_ref, bf16[10,4,32,1024]{3,2,1,0:T(8,128)(2,1)S(1)} %copy-done, f32[4,32,1024]{2,1,0:T(8,128)S(1)} %copy-done.1, bf16[96,128,128]{2,1,0:T(8,128)(2,1)} %loc_hbm.1), custom_call_target="tpu_custom_call" | custom-call | flops 2013265920 | bytes 6291456 | tf_op jit(solution)/shard_map/pallas_call | solution.py:297
  38.9 0.7 %copy.9 = f32[4,32,512]{2,1,0:T(8,128)} copy(f32[4,32,512]{2,1,0:T(8,128)S(1)} %shard_map.64) | data formatting | bytes 524288
  (2 shorter events, 0.0 us)
Async XLA Ops:
  1.1 1.7 %copy-start = (bf16[10,4,32,1024]{3,2,1,0:T(8,128)(2,1)S(1)}, bf16[10,4,32,1024]{3,2,1,0:T(8,128)(2,1)}, u32[]{:S(2)}) copy-start(bf16[10,4,32,1024]{3,2,1,0:T(8,128)(2,1)} %ens_hbm.1) | copy-start | bytes 7864324
  2.9 1.0 %copy-start.1 = (f32[4,32,1024]{2,1,0:T(8,128)S(1)}, f32[4,32,1024]{2,1,0:T(8,128)}, u32[]{:S(2)}) copy-start(f32[4,32,1024]{2,1,0:T(8,128)} %control_hbm.1) | copy-start | bytes 1572868
  3.9 0.7 %copy-start.2 = (s32[8]{0:T(128)S(1)}, s32[8]{0:T(128)}, u32[]{:S(2)}) copy-start(s32[8]{0:T(128)} %count_ref.1) | copy-start | bytes 100
  4.6 0.7 %copy-start.3 = (s32[32]{0:T(128)S(1)}, s32[32]{0:T(128)}, u32[]{:S(2)}) copy-start(s32[32]{0:T(128)} %level_ref.1) | copy-start | bytes 388

commit v2 on v1

v2 whole, which is shorter than its diff:
```python
import functools

import jax
import jax.numpy as jnp
from jax import lax
from jax.experimental import pallas as pl
from jax.experimental.pallas import tpu as pltpu
from jax.sharding import PartitionSpec as P

SPAN = 12
MESH = pl.DeviceIdType.MESH


vertical_scale = 8.0


def kernel(
    sizes,
    count_hbm,
    level_hbm,
    pair_hbm,
    ens_hbm,
    control_hbm,
    loc_hbm,
    out_ref,
    counts,
    level_at,
    listed,
    slot,
    ens,
    control,
    loc,
    table,
    far,
    relay_in,
    near_in,
    spread,
    terms,
    terms_in,
    small_sems,
    in_sems,
    lift_send,
    lift_recv,
    far_send,
    far_recv,
    term_send,
    term_recv,
):
    members, slots, levels, own, width, devices, peers = sizes
    extra = SPAN - own
    pairs = loc_hbm.shape[0]
    per_block = pairs // own
    here = lax.axis_index("grid")
    mem = lax.axis_index("mem")
    up = lax.rem(here + 1, devices)
    down = lax.rem(here + devices - 1, devices)
    parts = own // 2

    def cols(first, last):
        return slice(first * width, last * width)

    small = [
        pltpu.make_async_copy(level_hbm, level_at, small_sems.at[0]),
        pltpu.make_async_copy(count_hbm, counts, small_sems.at[1]),
        pltpu.make_async_copy(pair_hbm, listed, small_sems.at[2]),
    ]
    for copy in small:
        copy.start()
    loads = []
    for part in range(parts):
        at = cols(2 * part, 2 * part + 2)
        a = pltpu.make_async_copy(
            control_hbm.at[:, :, at], control.at[:, :, at], in_sems.at[2 * part]
        )
        b = pltpu.make_async_copy(
            ens_hbm.at[:, :, :, at], ens.at[:, :, :, at], in_sems.at[2 * part + 1]
        )
        a.start()
        b.start()
        loads.append((a, b))
    load_loc = pltpu.make_async_copy(loc_hbm, loc.at[pl.ds(0, pairs)], in_sems.at[2 * parts])
    load_loc.start()

    barrier = pltpu.get_barrier_semaphore()
    for other in (up, down):
        pl.semaphore_signal(barrier, inc=1, device_id={"grid": other}, device_id_type=MESH)
    for away in range(1, peers):
        pl.semaphore_signal(
            barrier, inc=1, device_id={"mem": lax.rem(mem + away, peers)}, device_id_type=MESH
        )

    loc[pairs] = jnp.zeros((width, width), loc.dtype)

    group = max(g for g in range(1, members + 1) if members % g == 0 and g * levels <= 256)
    size = group * levels
    down_at = lax.broadcasted_iota(jnp.int32, (size, 1), 0)
    across_at = lax.broadcasted_iota(jnp.int32, (1, size), 1)
    level_down = jnp.zeros((size, 1), jnp.float32)
    level_across = jnp.zeros((1, size), jnp.float32)
    for copy in small:
        copy.wait()
    for l in range(levels):
        value = level_at[l].astype(jnp.float32)
        level_down = jnp.where(down_at % levels == l, value, level_down)
        level_across = jnp.where(across_at % levels == l, value, level_across)
    vert = jnp.exp(-jnp.abs(level_down - level_across) / vertical_scale)
    vert = jnp.where(down_at // levels == across_at // levels, vert, 0.0)

    low = 7
    for b in range(own):
        first_word = jnp.int32(0)
        second_word = jnp.int32(0)
        for p in range(per_block):
            k = listed[1, b * per_block + p] - listed[0, b * per_block + p]
            k = jnp.where(k < 0, k + own * devices, k)
            near = k < low
            code = jnp.int32(p + 1) << (4 * jnp.where(near, k, k - low))
            first_word = first_word + jnp.where(near, code, 0)
            second_word = second_word + jnp.where(near, 0, code)
        for k in range(SPAN + 1):
            word = first_word >> (4 * k) if k < low else second_word >> (4 * (k - low))
            place = word & 15
            at = jnp.minimum(b * per_block + place - 1, pairs)
            slot[b * (SPAN + 1) + k] = jnp.where(place == 0, pairs, at)

    lane = lax.broadcasted_iota(jnp.int32, (1, width), 1)

    def live(block):
        return (lane < counts[block]).astype(jnp.float32)

    def lift_copy(which, src, dst, n):
        return pltpu.make_async_remote_copy(
            src_ref=table.at[:, cols(src, src + n)],
            dst_ref=table.at[:, cols(dst, dst + n)],
            send_sem=lift_send.at[which],
            recv_sem=lift_recv.at[which],
            device_id={"grid": down},
            device_id_type=MESH,
        )

    lift_own = [lift_copy(part, 2 * part, own + 2 * part, 2) for part in range(parts)]
    lift_relay = [lift_copy(parts + n, own + n, 2 * own + n, 1) for n in range(extra)]

    def far_copy(which, src, dst_ref, n):
        return pltpu.make_async_remote_copy(
            src_ref=far.at[:, cols(src, src + n)],
            dst_ref=dst_ref,
            send_sem=far_send.at[which],
            recv_sem=far_recv.at[which],
            device_id={"grid": up},
            device_id_type=MESH,
        )

    far_two = {
        n: far_copy(n // 2, own + n, relay_in.at[:, cols(n, n + 2)], 2)
        for n in range(0, extra, 2)
    }
    far_mid = {
        n: far_copy(n // 2, n, near_in.at[:, cols(n, n + 2)], 2) for n in range(extra, own, 2)
    }
    far_last = [
        far_copy(parts + n, n, near_in.at[:, cols(n, n + 1)], 1) for n in range(extra)
    ]

    def pair(i, k, least):
        return loc[slot[i * (SPAN + 1) + k] if least <= k <= SPAN else pairs]

    def from_below(j, n, first, last):
        stack = jnp.concatenate(
            [
                jnp.concatenate([pair(i, j + c - i, 1) for i in range(first, last)], axis=0)
                for c in range(n)
            ],
            axis=1,
        )
        return jnp.dot(table[:, cols(first, last)], stack, preferred_element_type=jnp.float32)

    def from_above(j, n, first, last):
        stack = jnp.concatenate(
            [
                jnp.concatenate([pair(j + c, s - j - c, 0) for s in range(first, last)], axis=1)
                for c in range(n)
            ],
            axis=0,
        )
        return lax.dot_general(
            table[:, cols(first, last)],
            stack,
            (((1,), (1,)), ((), ())),
            preferred_element_type=jnp.float32,
        )

    def lift(part):
        loads[part][0].wait()
        loads[part][1].wait()
        at = cols(2 * part, 2 * part + 2)
        mask = jnp.concatenate([live(2 * part), live(2 * part + 1)], axis=1)
        masked = [control[t, :, at] * mask for t in range(slots)]
        for g in range(members // group):
            weighted = []
            for m in range(g * group, (g + 1) * group):
                total = ens[m, 0, :, at].astype(jnp.float32) * masked[0]
                for t in range(1, slots):
                    total = total + ens[m, t, :, at].astype(jnp.float32) * masked[t]
                weighted.append(total)
            lifted = jnp.dot(
                vert,
                jnp.concatenate(weighted, axis=0),
                precision=lax.Precision.HIGHEST,
                preferred_element_type=jnp.float32,
            )
            table[g * size : (g + 1) * size, at] = lifted.astype(table.dtype)

    for part in range(parts):
        lift(part)
        if part == 0:
            pl.semaphore_wait(barrier, 2 + peers - 1)
        lift_own[part].start()
    load_loc.wait()

    for n in range(0, extra, 2):
        j = 2 * own + n
        far[:, cols(j - own, j - own + 2)] = from_below(j, 2, j - SPAN, own).astype(far.dtype)
        far_two[n].start()
    for n in range(extra, own, 2):
        j = own + n
        far[:, cols(n, n + 2)] = from_below(j, 2, j - SPAN, own).astype(far.dtype)
        far_mid[n].start()

    for part in range(extra // 2):
        lift_own[part].wait_recv()
        for n in (2 * part, 2 * part + 1):
            lift_relay[n].start()

    for n in range(0, extra, 2):
        far_two[n].wait_recv()
        j = own + n
        total = from_below(j, 2, max(0, j - SPAN), own)
        total = total + relay_in[:, cols(n, n + 2)].astype(jnp.float32)
        far[:, cols(n, n + 2)] = total.astype(far.dtype)
        far_last[n].start()
        far_last[n + 1].start()

    for j in range(0, own, 2):
        spread[:, cols(j, j + 2)] = from_above(j, 2, j, own) + from_below(j, 2, 0, j + 1)

    for part in range(parts):
        if part >= extra // 2:
            lift_own[part].wait_recv()
        source = own + 2 * part
        for j in range(0, own, 2):
            if source <= j + 1 + SPAN:
                spread[:, cols(j, j + 2)] += from_above(j, 2, source, source + 2)

    chunk = own // peers

    def finish(j):
        column = cols(j, j + 1)
        total = spread[:, column] + near_in[:, column].astype(jnp.float32)
        if j + SPAN >= 2 * own:
            total = total + from_above(j, 1, 2 * own, j + SPAN + 1)
        scale = live(j) / (members * peers - 1)
        for t in range(slots):
            mixed = ens[0, t, :, column].astype(jnp.float32) * total[:levels]
            for m in range(1, members):
                mixed = mixed + ens[m, t, :, column].astype(jnp.float32) * (
                    total[m * levels : (m + 1) * levels]
                )
            terms[j, t] = mixed * scale
        to = j // chunk

        @pl.when(mem != to)
        def _():
            pltpu.make_async_remote_copy(
                src_ref=terms.at[j],
                dst_ref=terms_in.at[mem, j % chunk],
                send_sem=term_send.at[j],
                recv_sem=term_recv.at[mem, j % chunk],
                device_id={"mem": jnp.int32(to)},
                device_id_type=MESH,
            ).start()

        @pl.when(mem == to)
        def _():
            terms_in[to, j % chunk] = terms[j]

    waiting = dict(far_mid)
    for n in range(max(extra, own - extra)):
        j = extra + n
        if j < own:
            if j in waiting:
                waiting.pop(j).wait_recv()
            if j + SPAN >= 2 * own:
                lift_relay[j + SPAN - 2 * own].wait_recv()
            finish(j)
        if n < extra:
            far_last[n].wait_recv()
            finish(n)

    for q in range(chunk):
        for source in range(peers):

            @pl.when(mem != source)
            def _():
                pltpu.make_async_remote_copy(
                    src_ref=terms.at[source * chunk + q],
                    dst_ref=terms_in.at[source, q],
                    send_sem=term_send.at[source * chunk + q],
                    recv_sem=term_recv.at[source, q],
                    device_id={"mem": jnp.int32(source)},
                    device_id_type=MESH,
                ).wait()

        result = terms_in[0, q]
        for source in range(1, peers):
            result = result + terms_in[source, q]
        out_ref[:, :, cols(q, q + 1)] = result
    for copy in (
        lift_own + lift_relay + list(far_two.values()) + list(far_mid.values()) + far_last
    ):
        copy.wait_send()


def per_device(ens, control, col_count, level_index, pair_blocks, loc_blocks):
    own = col_count.shape[0]
    width = loc_blocks.shape[1]
    pairs = pair_blocks.shape[0]
    devices = lax.axis_size("grid")
    peers = lax.axis_size("mem")
    members, slots, levels, columns = ens.shape
    rows = members * levels
    extra = SPAN - own
    assert 0 < extra <= own and own % peers == 0 and devices > 2
    assert own % 2 == 0 and extra % 2 == 0 and pairs // own < 16

    parts = own // 2
    chunk = own // peers
    sizes = (members, slots, levels, own, width, devices, peers)
    dma = pltpu.SemaphoreType.DMA
    return pl.pallas_call(
        functools.partial(kernel, sizes),
        out_shape=jax.ShapeDtypeStruct((slots, levels, columns // peers), jnp.float32),
        in_specs=[pl.BlockSpec(memory_space=pltpu.HBM)] * 6,
        out_specs=pl.BlockSpec(memory_space=pltpu.VMEM),
        scratch_shapes=[
            pltpu.SMEM(col_count.shape, jnp.int32),
            pltpu.SMEM(level_index.shape, jnp.int32),
            pltpu.SMEM((2, pairs), jnp.int32),
            pltpu.SMEM((own * (SPAN + 1),), jnp.int32),
            pltpu.VMEM(ens.shape, ens.dtype),
            pltpu.VMEM(control.shape, control.dtype),
            pltpu.VMEM((pairs + 1, width, width), loc_blocks.dtype),
            pltpu.VMEM((rows, (own + SPAN) * width), jnp.bfloat16),
            pltpu.VMEM((rows, SPAN * width), jnp.bfloat16),
            pltpu.VMEM((rows, extra * width), jnp.bfloat16),
            pltpu.VMEM((rows, columns), jnp.bfloat16),
            pltpu.VMEM((rows, columns), jnp.float32),
            pltpu.VMEM((own, slots, levels, width), jnp.float32),
            pltpu.VMEM((peers, chunk, slots, levels, width), jnp.float32),
            dma((3,)),
            dma((2 * parts + 1,)),
            dma((parts + extra,)),
            dma((parts + extra,)),
            dma((parts + extra,)),
            dma((parts + extra,)),
            dma((own,)),
            dma((peers, chunk)),
        ],
        compiler_params=pltpu.CompilerParams(
            collective_id=0, has_side_effects=True, vmem_limit_bytes=56 * 1024 * 1024
        ),
        cost_estimate=pl.CostEstimate(
            flops=2 * rows * width * width * pairs * 2,
            bytes_accessed=ens.size * 2 + control.size * 4 + loc_blocks.size * 2,
            transcendentals=0,
        ),
    )(col_count, level_index, pair_blocks.T, ens, control, loc_blocks)


def solution(mesh):
    return jax.shard_map(
        per_device,
        mesh=mesh,
        in_specs=(
            P("mem", None, None, "grid"),
            P(None, None, "grid"),
            P("grid"),
            P(),
            P("grid", None),
            P("grid", None, None),
        ),
        out_specs=P(None, None, ("grid", "mem")),
        check_vma=False,
    )
```

time: 39.9 us -> 33.4 us (0.84)
  local copies, waits for them, and re-layouts: 5.04 us -> 1.67 us
  Pallas kernels: 33.7 us -> 31.4 us
  other arithmetic: 0.89 us -> 0 us
    unnamed x9 -> x1, local copies, waits for them, and re-layouts: 4.8 us -> 1.67 us
    pallas_call x1, Pallas kernels: 33.7 us -> 31.4 us  [per_device(): pl.pallas_call(functools.partial(kernel, sizes), out_shape=jax.ShapeDtype...]
    sub x1 -> x0, other arithmetic: 0.77 us -> none  [per_device(): offsets = jnp.mod(pair_blocks[:, 1] - pair_blocks[:, 0], own * devices)]
where the time goes in v2:
time: 33.4 us; the launch traced here: 33.1 us
  Pallas kernels  31.4 us (94%)
  local copies, waits for them, and re-layouts  1.67 us (5%)
    pallas_call x1, Pallas kernels, per_device(): pl.pallas_call(functools.partial(kernel, sizes), out_shape=jax.ShapeDtype...  31.4 us
    unnamed x1, local copies, waits for them, and re-layouts  1.67 us

profile of v2, /device:TPU:26, one launch (start us, length us, event | category | flops | bytes accessed | tf_op | source)
XLA Modules:
  0.0 33.1 jit_solution(4757869774217852226)
XLA Ops:
  0.0 31.4 %shard_map.64 = f32[4,32,512]{2,1,0:T(8,128)} custom-call(s32[8]{0:T(128)} %count_hbm.1, s32[32]{0:T(128)} %level_hbm.1, s32[2,96]{1,0:T(2,128)} %bitcast.1, bf16[10,4,32,1024]{3,2,1,0:T(8,128)(2,1)} %ens_hbm.1, f32[4,32,1024]{2,1,0:T(8,128)} %control_hbm.1, bf16[96,128,128]{2,1,0:T(8,128)(2,1)} %loc_hbm.1), custom_call_target="tpu_custom_call" | custom-call | flops 2013265920 | bytes 6291456 | tf_op jit(solution)/shard_map/pallas_call | solution.py:340
  31.4 1.7 %copy.8 = f32[4,32,512]{2,1,0:T(8,128)} copy(f32[4,32,512]{2,1,0:T(8,128)} %shard_map.64) | data formatting | bytes 524288

commit v3 on v2

v3 whole, which is shorter than its diff:
```python
import functools

import jax
import jax.numpy as jnp
from jax import lax
from jax.experimental import pallas as pl
from jax.experimental.pallas import tpu as pltpu
from jax.sharding import PartitionSpec as P

SPAN = 12
MESH = pl.DeviceIdType.MESH


vertical_scale = 8.0


def pieces_of(own):
    return [(0, 1), (1, 1)] + [(first, 2) for first in range(2, own, 2)]


def kernel(
    sizes,
    count_hbm,
    level_hbm,
    pair_hbm,
    ens_hbm,
    control_hbm,
    loc_hbm,
    out_ref,
    counts,
    level_at,
    listed,
    slot,
    ens,
    control,
    loc,
    table,
    far,
    relay_in,
    near_in,
    spread,
    terms,
    terms_in,
    small_sems,
    loc_sem,
    in_sems,
    lift_send,
    lift_recv,
    far_send,
    far_recv,
    term_send,
    term_recv,
):
    members, slots, levels, own, width, devices, peers = sizes
    extra = SPAN - own
    pairs = loc_hbm.shape[0]
    per_block = pairs // own
    here = lax.axis_index("grid")
    mem = lax.axis_index("mem")
    up = lax.rem(here + 1, devices)
    down = lax.rem(here + devices - 1, devices)
    pieces = pieces_of(own)

    def cols(first, last):
        return slice(first * width, last * width)

    small = [
        pltpu.make_async_copy(level_hbm, level_at, small_sems.at[0]),
        pltpu.make_async_copy(count_hbm, counts, small_sems.at[1]),
    ]
    load_pairs = pltpu.make_async_copy(pair_hbm, listed, small_sems.at[2])
    load_loc = pltpu.make_async_copy(loc_hbm, loc.at[pl.ds(0, pairs)], loc_sem)
    loads = {}
    for first, n in pieces:
        at = cols(first, first + n)
        loads[first] = (
            pltpu.make_async_copy(
                control_hbm.at[:, :, at], control.at[:, :, at], in_sems.at[2 * first]
            ),
            pltpu.make_async_copy(
                ens_hbm.at[:, :, :, at], ens.at[:, :, :, at], in_sems.at[2 * first + 1]
            ),
        )
    for copy in small:
        copy.start()
    for first, n in pieces[:2]:
        for copy in loads[first]:
            copy.start()

    barrier = pltpu.get_barrier_semaphore()
    for other in (up, down):
        pl.semaphore_signal(barrier, inc=1, device_id={"grid": other}, device_id_type=MESH)
    for away in range(1, peers):
        pl.semaphore_signal(
            barrier, inc=1, device_id={"mem": lax.rem(mem + away, peers)}, device_id_type=MESH
        )

    loc[pairs] = jnp.zeros((width, width), loc.dtype)

    group = max(g for g in range(1, members + 1) if members % g == 0 and g * levels <= 256)
    size = group * levels
    down_at = lax.broadcasted_iota(jnp.int32, (size, 1), 0)
    across_at = lax.broadcasted_iota(jnp.int32, (1, size), 1)
    level_down = jnp.zeros((size, 1), jnp.float32)
    level_across = jnp.zeros((1, size), jnp.float32)
    for copy in small:
        copy.wait()
    for l in range(levels):
        value = level_at[l].astype(jnp.float32)
        level_down = jnp.where(down_at % levels == l, value, level_down)
        level_across = jnp.where(across_at % levels == l, value, level_across)
    vert = jnp.exp(-jnp.abs(level_down - level_across) / vertical_scale)
    vert = jnp.where(down_at // levels == across_at // levels, vert, 0.0)

    lane = lax.broadcasted_iota(jnp.int32, (1, width), 1)

    def live(block):
        return (lane < counts[block]).astype(jnp.float32)

    def lift_copy(which, src, dst, n):
        return pltpu.make_async_remote_copy(
            src_ref=table.at[pl.ds(src, n)],
            dst_ref=table.at[pl.ds(dst, n)],
            send_sem=lift_send.at[which],
            recv_sem=lift_recv.at[which],
            device_id={"grid": down},
            device_id_type=MESH,
        )

    lift_own = {first: lift_copy(first, first, own + first, n) for first, n in pieces}
    lift_relay = [lift_copy(own + n, own + n, 2 * own + n, 1) for n in range(extra)]
    due = dict(lift_own)

    def arrive(last):
        for first in [f for f in due if f < last]:
            due.pop(first).wait_recv()

    def far_copy(which, src, dst_ref, n):
        return pltpu.make_async_remote_copy(
            src_ref=far.at[pl.ds(src, n)],
            dst_ref=dst_ref,
            send_sem=far_send.at[which],
            recv_sem=far_recv.at[which],
            device_id={"grid": up},
            device_id_type=MESH,
        )

    far_two = {
        n: far_copy(own + n, own + n, relay_in.at[pl.ds(n, 2)], 2) for n in range(0, extra, 2)
    }
    far_mid = {n: far_copy(n, n, near_in.at[pl.ds(n, 2)], 2) for n in range(extra, own, 2)}
    far_last = [far_copy(n, n, near_in.at[pl.ds(n, 1)], 1) for n in range(extra)]

    def pair(i, k, least):
        return loc[slot[i * (SPAN + 1) + k] if least <= k <= SPAN else pairs]

    def blocks(first, last):
        return jnp.concatenate([table[b] for b in range(first, last)], axis=1)

    def from_below(j, n, first, last):
        stack = jnp.concatenate(
            [
                jnp.concatenate([pair(i, j + c - i, 1) for i in range(first, last)], axis=0)
                for c in range(n)
            ],
            axis=1,
        )
        return jnp.dot(blocks(first, last), stack, preferred_element_type=jnp.float32)

    def from_above(j, n, first, last):
        stack = jnp.concatenate(
            [
                jnp.concatenate([pair(j + c, s - j - c, 0) for s in range(first, last)], axis=1)
                for c in range(n)
            ],
            axis=0,
        )
        return lax.dot_general(
            blocks(first, last),
            stack,
            (((1,), (1,)), ((), ())),
            preferred_element_type=jnp.float32,
        )

    def lift(first, n):
        for copy in loads[first]:
            copy.wait()
        at = cols(first, first + n)
        mask = jnp.concatenate([live(first + c) for c in range(n)], axis=1)
        masked = [control[t, :, at] * mask for t in range(slots)]
        for g in range(members // group):
            weighted = []
            for m in range(g * group, (g + 1) * group):
                total = ens[m, 0, :, at].astype(jnp.float32) * masked[0]
                for t in range(1, slots):
                    total = total + ens[m, t, :, at].astype(jnp.float32) * masked[t]
                weighted.append(total)
            lifted = jnp.dot(
                vert,
                jnp.concatenate(weighted, axis=0),
                precision=lax.Precision.HIGHEST,
                preferred_element_type=jnp.float32,
            )
            for c in range(n):
                table[first + c, g * size : (g + 1) * size] = lifted[:, cols(c, c + 1)].astype(
                    table.dtype
                )

    for first, n in pieces:
        lift(first, n)
        if first == 0:
            for later, n in pieces[2:]:
                for copy in loads[later]:
                    copy.start()
            load_pairs.start()
            load_loc.start()
            pl.semaphore_wait(barrier, 2 + peers - 1)
        lift_own[first].start()

    load_pairs.wait()
    low = 7
    for b in range(own):
        first_word = jnp.int32(0)
        second_word = jnp.int32(0)
        for p in range(per_block):
            k = listed[1, b * per_block + p] - listed[0, b * per_block + p]
            k = jnp.where(k < 0, k + own * devices, k)
            near = k < low
            code = jnp.int32(p + 1) << (4 * jnp.where(near, k, k - low))
            first_word = first_word + jnp.where(near, code, 0)
            second_word = second_word + jnp.where(near, 0, code)
        for k in range(SPAN + 1):
            word = first_word >> (4 * k) if k < low else second_word >> (4 * (k - low))
            place = word & 15
            at = jnp.minimum(b * per_block + place - 1, pairs)
            slot[b * (SPAN + 1) + k] = jnp.where(place == 0, pairs, at)

    load_loc.wait()

    def keep_far(at, total):
        for c in range(2):
            far[at + c] = total[:, cols(c, c + 1)].astype(far.dtype)

    for n in range(0, extra, 2):
        j = 2 * own + n
        keep_far(own + n, from_below(j, 2, j - SPAN, own))
        far_two[n].start()
    for n in range(extra, own, 2):
        j = own + n
        keep_far(n, from_below(j, 2, j - SPAN, own))
        far_mid[n].start()

    for n in range(extra):
        arrive(n + 1)
        lift_relay[n].start()

    for n in range(0, extra, 2):
        j = own + n
        total = from_below(j, 2, max(0, j - SPAN), own)
        far_two[n].wait_recv()
        passing = jnp.concatenate([relay_in[n], relay_in[n + 1]], axis=1)
        keep_far(n, total + passing.astype(jnp.float32))
        far_last[n].start()
        far_last[n + 1].start()

    for j in range(0, own, 2):
        spread[:, cols(j, j + 2)] = from_above(j, 2, j, own) + from_below(j, 2, 0, j + 1)

    for first in range(0, own, 2):
        arrive(first + 2)
        source = own + first
        for j in range(0, own, 2):
            if source <= j + 1 + SPAN:
                spread[:, cols(j, j + 2)] += from_above(j, 2, source, source + 2)

    chunk = own // peers

    def finish(j):
        column = cols(j, j + 1)
        total = spread[:, column] + near_in[j].astype(jnp.float32)
        if j + SPAN >= 2 * own:
            total = total + from_above(j, 1, 2 * own, j + SPAN + 1)
        scale = live(j) / (members * peers - 1)
        for t in range(slots):
            mixed = ens[0, t, :, column].astype(jnp.float32) * total[:levels]
            for m in range(1, members):
                mixed = mixed + ens[m, t, :, column].astype(jnp.float32) * (
                    total[m * levels : (m + 1) * levels]
                )
            terms[j, t] = mixed * scale
        to = j // chunk

        @pl.when(mem != to)
        def _():
            pltpu.make_async_remote_copy(
                src_ref=terms.at[j],
                dst_ref=terms_in.at[mem, j % chunk],
                send_sem=term_send.at[j],
                recv_sem=term_recv.at[mem, j % chunk],
                device_id={"mem": jnp.int32(to)},
                device_id_type=MESH,
            ).start()

        @pl.when(mem == to)
        def _():
            terms_in[to, j % chunk] = terms[j]

    waiting = dict(far_mid)
    for n in range(max(extra, own - extra)):
        j = extra + n
        if j < own:
            if j in waiting:
                waiting.pop(j).wait_recv()
            if j + SPAN >= 2 * own:
                lift_relay[j + SPAN - 2 * own].wait_recv()
            finish(j)
        if n < extra:
            far_last[n].wait_recv()
            finish(n)

    for q in range(chunk):
        for source in range(peers):

            @pl.when(mem != source)
            def _():
                pltpu.make_async_remote_copy(
                    src_ref=terms.at[source * chunk + q],
                    dst_ref=terms_in.at[source, q],
                    send_sem=term_send.at[source * chunk + q],
                    recv_sem=term_recv.at[source, q],
                    device_id={"mem": jnp.int32(source)},
                    device_id_type=MESH,
                ).wait()

        result = terms_in[0, q]
        for source in range(1, peers):
            result = result + terms_in[source, q]
        out_ref[:, :, cols(q, q + 1)] = result
    for copy in (
        list(lift_own.values()) + lift_relay + list(far_two.values()) + list(far_mid.values()) + far_last
    ):
        copy.wait_send()


def per_device(ens, control, col_count, level_index, pair_blocks, loc_blocks):
    own = col_count.shape[0]
    width = loc_blocks.shape[1]
    pairs = pair_blocks.shape[0]
    devices = lax.axis_size("grid")
    peers = lax.axis_size("mem")
    members, slots, levels, columns = ens.shape
    rows = members * levels
    extra = SPAN - own
    assert 0 < extra <= own and own % peers == 0 and devices > 2
    assert own % 2 == 0 and extra % 2 == 0 and pairs // own < 16

    chunk = own // peers
    sizes = (members, slots, levels, own, width, devices, peers)
    dma = pltpu.SemaphoreType.DMA
    return pl.pallas_call(
        functools.partial(kernel, sizes),
        out_shape=jax.ShapeDtypeStruct((slots, levels, columns // peers), jnp.float32),
        in_specs=[pl.BlockSpec(memory_space=pltpu.HBM)] * 6,
        out_specs=pl.BlockSpec(memory_space=pltpu.VMEM),
        scratch_shapes=[
            pltpu.SMEM(col_count.shape, jnp.int32),
            pltpu.SMEM(level_index.shape, jnp.int32),
            pltpu.SMEM((2, pairs), jnp.int32),
            pltpu.SMEM((own * (SPAN + 1),), jnp.int32),
            pltpu.VMEM(ens.shape, ens.dtype),
            pltpu.VMEM(control.shape, control.dtype),
            pltpu.VMEM((pairs + 1, width, width), loc_blocks.dtype),
            pltpu.VMEM((own + SPAN, rows, width), jnp.bfloat16),
            pltpu.VMEM((SPAN, rows, width), jnp.bfloat16),
            pltpu.VMEM((extra, rows, width), jnp.bfloat16),
            pltpu.VMEM((own, rows, width), jnp.bfloat16),
            pltpu.VMEM((rows, columns), jnp.float32),
            pltpu.VMEM((own, slots, levels, width), jnp.float32),
            pltpu.VMEM((peers, chunk, slots, levels, width), jnp.float32),
            dma((3,)),
            dma,
            dma((2 * own,)),
            dma((SPAN,)),
            dma((SPAN,)),
            dma((SPAN,)),
            dma((SPAN,)),
            dma((own,)),
            dma((peers, chunk)),
        ],
        compiler_params=pltpu.CompilerParams(
            collective_id=0, has_side_effects=True, vmem_limit_bytes=56 * 1024 * 1024
        ),
        cost_estimate=pl.CostEstimate(
            flops=2 * rows * width * width * pairs * 2,
            bytes_accessed=ens.size * 2 + control.size * 4 + loc_blocks.size * 2,
            transcendentals=0,
        ),
    )(col_count, level_index, pair_blocks.T, ens, control, loc_blocks)


def solution(mesh):
    return jax.shard_map(
        per_device,
        mesh=mesh,
        in_specs=(
            P("mem", None, None, "grid"),
            P(None, None, "grid"),
            P("grid"),
            P(),
            P("grid", None),
            P("grid", None, None),
        ),
        out_specs=P(None, None, ("grid", "mem")),
        check_vma=False,
    )
```

time: 33.4 us -> 33.9 us (1.015)
  Pallas kernels: 31.4 us -> 32.1 us
    pallas_call x1, Pallas kernels: 31.4 us -> 32.1 us  [per_device(): pl.pallas_call(functools.partial(kernel, sizes), out_shape=jax.ShapeDtype...]
where the time goes in v3:
time: 33.9 us; the launch traced here: 33.8 us
  Pallas kernels  32.1 us (95%)
  local copies, waits for them, and re-layouts  1.67 us (5%)
    pallas_call x1, Pallas kernels, per_device(): pl.pallas_call(functools.partial(kernel, sizes), out_shape=jax.ShapeDtype...  32.1 us
    unnamed x1, local copies, waits for them, and re-layouts  1.67 us

profile of v3, /device:TPU:26, one launch (start us, length us, event | category | flops | bytes accessed | tf_op | source)
XLA Modules:
  0.0 33.8 jit_solution(13905348243480636761)
XLA Ops:
  0.0 32.1 %shard_map.64 = f32[4,32,512]{2,1,0:T(8,128)} custom-call(s32[8]{0:T(128)} %count_hbm.1, s32[32]{0:T(128)} %level_hbm.1, s32[2,96]{1,0:T(2,128)} %bitcast.1, bf16[10,4,32,1024]{3,2,1,0:T(8,128)(2,1)} %ens_hbm.1, f32[4,32,1024]{2,1,0:T(8,128)} %control_hbm.1, bf16[96,128,128]{2,1,0:T(8,128)(2,1)} %loc_hbm.1), custom_call_target="tpu_custom_call" | custom-call | flops 2013265920 | bytes 6291456 | tf_op jit(solution)/shard_map/pallas_call | solution.py:360
  32.1 1.7 %copy.8 = f32[4,32,512]{2,1,0:T(8,128)} copy(f32[4,32,512]{2,1,0:T(8,128)} %shard_map.64) | data formatting | bytes 524288

commit v4 on v3

--- a/solution.py
+++ b/solution.py
@@ -357,6 +357,7 @@
     chunk = own // peers
     sizes = (members, slots, levels, own, width, devices, peers)
     dma = pltpu.SemaphoreType.DMA
+    operands = (col_count, level_index, pair_blocks.T, ens, control, loc_blocks)
     return pl.pallas_call(
         functools.partial(kernel, sizes),
         out_shape=jax.ShapeDtypeStruct((slots, levels, columns // peers), jnp.float32),
@@ -388,14 +389,14 @@
             dma((peers, chunk)),
         ],
         compiler_params=pltpu.CompilerParams(
-            collective_id=0, has_side_effects=True, vmem_limit_bytes=56 * 1024 * 1024
+            collective_id=0, has_side_effects=True, vmem_limit_bytes=32 * 1024 * 1024
         ),
         cost_estimate=pl.CostEstimate(
             flops=2 * rows * width * width * pairs * 2,
             bytes_accessed=ens.size * 2 + control.size * 4 + loc_blocks.size * 2,
             transcendentals=0,
         ),
-    )(col_count, level_index, pair_blocks.T, ens, control, loc_blocks)
+    )(*[pltpu.with_memory_space_constraint(array, pltpu.HBM) for array in operands])
 
 
 def solution(mesh):

time: 33.9 us -> 32.3 us (0.953)
  local copies, waits for them, and re-layouts: 1.67 us -> 0.71 us
  Pallas kernels: 32.1 us -> 31.4 us
    unnamed x1, local copies, waits for them, and re-layouts: 1.67 us -> 0.71 us
    pallas_call x1, Pallas kernels: 32.1 us -> 31.4 us  [per_device(): pl.pallas_call(functools.partial(kernel, sizes), out_shape=jax.ShapeDtype...]
where the time goes in v4:
time: 32.3 us; the launch traced here: 32.1 us
  Pallas kernels  31.4 us (97%)
  local copies, waits for them, and re-layouts  0.71 us (2%)
    pallas_call x1, Pallas kernels, per_device(): pl.pallas_call(functools.partial(kernel, sizes), out_shape=jax.ShapeDtype...  31.4 us
    unnamed x1, local copies, waits for them, and re-layouts  0.71 us

profile of v4, /device:TPU:26, one launch (start us, length us, event | category | flops | bytes accessed | tf_op | source)
XLA Modules:
  0.0 32.1 jit_solution(7313569573701550899)
XLA Ops:
  0.0 31.4 %shard_map.64 = f32[4,32,512]{2,1,0:T(8,128)S(1)} custom-call(s32[8]{0:T(128)} %count_hbm.1, s32[32]{0:T(128)} %level_hbm.1, s32[2,96]{1,0:T(2,128)} %bitcast.1, bf16[10,4,32,1024]{3,2,1,0:T(8,128)(2,1)} %ens_hbm.1, f32[4,32,1024]{2,1,0:T(8,128)} %control_hbm.1, bf16[96,128,128]{2,1,0:T(8,128)(2,1)} %loc_hbm.1), custom_call_target="tpu_custom_call" | custom-call | flops 2013265920 | bytes 6291456 | tf_op jit(solution)/shard_map/pallas_call | solution.py:361
  31.4 0.7 %copy.8 = f32[4,32,512]{2,1,0:T(8,128)} copy(f32[4,32,512]{2,1,0:T(8,128)S(1)} %shard_map.64) | data formatting | bytes 524288

commit v5 on v4

--- a/solution.py
+++ b/solution.py
@@ -15,7 +15,11 @@
 
 
 def pieces_of(own):
-    return [(0, 1), (1, 1)] + [(first, 2) for first in range(2, own, 2)]
+    return [(first, 2) for first in range(0, own, 2)]
+
+
+def messages_of(count):
+    return [(first, 2) for first in range(0, count - 2, 2)] + [(count - 2, 1), (count - 1, 1)]
 
 
 def kernel(
@@ -127,13 +131,21 @@
             device_id_type=MESH,
         )
 
-    lift_own = {first: lift_copy(first, first, own + first, n) for first, n in pieces}
-    lift_relay = [lift_copy(own + n, own + n, 2 * own + n, 1) for n in range(extra)]
+    near_part = [(first, 2) for first in range(0, extra, 2)]
+    far_part = [(extra, own - extra)] if own > extra else []
+    lift_own = {
+        first: lift_copy(first, first, own + first, n) for first, n in near_part + far_part
+    }
+    lift_relay = {
+        first: lift_copy(own + first, own + first, 2 * own + first, n)
+        for first, n in messages_of(extra)
+    }
     due = dict(lift_own)
-
-    def arrive(last):
-        for first in [f for f in due if f < last]:
-            due.pop(first).wait_recv()
+    due_relay = dict(lift_relay)
+
+    def arrive(last, waiting=due):
+        for first in [f for f in waiting if f < last]:
+            waiting.pop(first).wait_recv()
 
     def far_copy(which, src, dst_ref, n):
         return pltpu.make_async_remote_copy(
@@ -145,11 +157,16 @@
             device_id_type=MESH,
         )
 
-    far_two = {
-        n: far_copy(own + n, own + n, relay_in.at[pl.ds(n, 2)], 2) for n in range(0, extra, 2)
+    far_two = far_copy(own, own, relay_in, extra)
+    far_mid = {
+        first: far_copy(first, first, near_in.at[pl.ds(first, n)], n) for first, n in far_part
     }
-    far_mid = {n: far_copy(n, n, near_in.at[pl.ds(n, 2)], 2) for n in range(extra, own, 2)}
-    far_last = [far_copy(n, n, near_in.at[pl.ds(n, 1)], 1) for n in range(extra)]
+    far_last = {
+        first: far_copy(first, first, near_in.at[pl.ds(first, n)], n)
+        for first, n in messages_of(extra)
+    }
+    due_far = dict(far_last)
+    due_mid = dict(far_mid)
 
     def pair(i, k, least):
         return loc[slot[i * (SPAN + 1) + k] if least <= k <= SPAN else pairs]
@@ -209,12 +226,15 @@
     for first, n in pieces:
         lift(first, n)
         if first == 0:
-            for later, n in pieces[2:]:
+            for later, unused in pieces[2:]:
                 for copy in loads[later]:
                     copy.start()
             load_pairs.start()
             load_loc.start()
             pl.semaphore_wait(barrier, 2 + peers - 1)
+        if first in lift_own and first < extra:
+            lift_own[first].start()
+    for first, n in far_part:
         lift_own[first].start()
 
     load_pairs.wait()
@@ -244,24 +264,27 @@
     for n in range(0, extra, 2):
         j = 2 * own + n
         keep_far(own + n, from_below(j, 2, j - SPAN, own))
-        far_two[n].start()
+    far_two.start()
     for n in range(extra, own, 2):
         j = own + n
         keep_far(n, from_below(j, 2, j - SPAN, own))
-        far_mid[n].start()
-
-    for n in range(extra):
-        arrive(n + 1)
-        lift_relay[n].start()
+    for copy in far_mid.values():
+        copy.start()
+
+    for first, n in messages_of(extra):
+        arrive(first + n)
+        lift_relay[first].start()
 
     for n in range(0, extra, 2):
         j = own + n
         total = from_below(j, 2, max(0, j - SPAN), own)
-        far_two[n].wait_recv()
+        if n == 0:
+            far_two.wait_recv()
         passing = jnp.concatenate([relay_in[n], relay_in[n + 1]], axis=1)
         keep_far(n, total + passing.astype(jnp.float32))
-        far_last[n].start()
-        far_last[n + 1].start()
+        for at in (n, n + 1):
+            if at in far_last:
+                far_last[at].start()
 
     for j in range(0, own, 2):
         spread[:, cols(j, j + 2)] = from_above(j, 2, j, own) + from_below(j, 2, 0, j + 1)
@@ -305,18 +328,28 @@
         def _():
             terms_in[to, j % chunk] = terms[j]
 
-    waiting = dict(far_mid)
+    order = []
     for n in range(max(extra, own - extra)):
-        j = extra + n
-        if j < own:
-            if j in waiting:
-                waiting.pop(j).wait_recv()
-            if j + SPAN >= 2 * own:
-                lift_relay[j + SPAN - 2 * own].wait_recv()
-            finish(j)
-        if n < extra:
-            far_last[n].wait_recv()
-            finish(n)
+        order += [b for b in (extra + n, n) if extra <= b < own or b == n < extra]
+
+    def finish_after(j, relays, lasts):
+        if j >= extra:
+            arrive(j + 1, due_mid)
+            arrive(j + SPAN - 2 * own + 1, relays)
+        else:
+            arrive(j + 1, lasts)
+        finish(j)
+
+    for j in order[:-2]:
+        finish_after(j, due_relay, due_far)
+    first_core = lax.rem(here, 2) == 0
+    for turn, chosen in ((order[-2:], first_core), (order[:-3:-1], jnp.logical_not(first_core))):
+
+        @pl.when(chosen)
+        def _():
+            relays, lasts = dict(due_relay), dict(due_far)
+            for j in turn:
+                finish_after(j, relays, lasts)
 
     for q in range(chunk):
         for source in range(peers):
@@ -336,10 +369,10 @@
         for source in range(1, peers):
             result = result + terms_in[source, q]
         out_ref[:, :, cols(q, q + 1)] = result
-    for copy in (
-        list(lift_own.values()) + lift_relay + list(far_two.values()) + list(far_mid.values()) + far_last
-    ):
-        copy.wait_send()
+    for group_of in (lift_own, lift_relay, far_mid, far_last):
+        for copy in group_of.values():
+            copy.wait_send()
+    far_two.wait_send()
 
 
 def per_device(ens, control, col_count, level_index, pair_blocks, loc_blocks):

time: 32.3 us -> 32.6 us (level)
  Pallas kernels: 31.4 us -> 31.8 us
    pallas_call x1, Pallas kernels: 31.4 us -> 31.8 us  [per_device(): pl.pallas_call(functools.partial(kernel, sizes), out_shape=jax.ShapeDtype...]
where the time goes in v5:
time: 32.6 us; the launch traced here: 32.5 us
  Pallas kernels  31.8 us (98%)
  local copies, waits for them, and re-layouts  0.71 us (2%)
    pallas_call x1, Pallas kernels, per_device(): pl.pallas_call(functools.partial(kernel, sizes), out_shape=jax.ShapeDtype...  31.8 us
    unnamed x1, local copies, waits for them, and re-layouts  0.71 us

profile of v5, /device:TPU:26, one launch (start us, length us, event | category | flops | bytes accessed | tf_op | source)
XLA Modules:
  0.0 32.5 jit_solution(18134366658267809045)
XLA Ops:
  0.0 31.8 %shard_map.64 = f32[4,32,512]{2,1,0:T(8,128)S(1)} custom-call(s32[8]{0:T(128)} %count_hbm.1, s32[32]{0:T(128)} %level_hbm.1, s32[2,96]{1,0:T(2,128)} %bitcast.1, bf16[10,4,32,1024]{3,2,1,0:T(8,128)(2,1)} %ens_hbm.1, f32[4,32,1024]{2,1,0:T(8,128)} %control_hbm.1, bf16[96,128,128]{2,1,0:T(8,128)(2,1)} %loc_hbm.1), custom_call_target="tpu_custom_call" | custom-call | flops 2013265920 | bytes 6291456 | tf_op jit(solution)/shard_map/pallas_call | solution.py:394
  31.8 0.7 %copy.8 = f32[4,32,512]{2,1,0:T(8,128)} copy(f32[4,32,512]{2,1,0:T(8,128)S(1)} %shard_map.64) | data formatting | bytes 524288

commit v6 on v5

--- a/solution.py
+++ b/solution.py
@@ -19,7 +19,7 @@
 
 
 def messages_of(count):
-    return [(first, 2) for first in range(0, count - 2, 2)] + [(count - 2, 1), (count - 1, 1)]
+    return [(first, 1) for first in range(count)]
 
 
 def kernel(
@@ -132,7 +132,7 @@
         )
 
     near_part = [(first, 2) for first in range(0, extra, 2)]
-    far_part = [(extra, own - extra)] if own > extra else []
+    far_part = [(first, 2) for first in range(extra, own, 2)]
     lift_own = {
         first: lift_copy(first, first, own + first, n) for first, n in near_part + far_part
     }
@@ -232,9 +232,6 @@
             load_pairs.start()
             load_loc.start()
             pl.semaphore_wait(barrier, 2 + peers - 1)
-        if first in lift_own and first < extra:
-            lift_own[first].start()
-    for first, n in far_part:
         lift_own[first].start()
 
     load_pairs.wait()
@@ -268,8 +265,7 @@
     for n in range(extra, own, 2):
         j = own + n
         keep_far(n, from_below(j, 2, j - SPAN, own))
-    for copy in far_mid.values():
-        copy.start()
+        far_mid[n].start()
 
     for first, n in messages_of(extra):
         arrive(first + n)
@@ -301,8 +297,6 @@
     def finish(j):
         column = cols(j, j + 1)
         total = spread[:, column] + near_in[j].astype(jnp.float32)
-        if j + SPAN >= 2 * own:
-            total = total + from_above(j, 1, 2 * own, j + SPAN + 1)
         scale = live(j) / (members * peers - 1)
         for t in range(slots):
             mixed = ens[0, t, :, column].astype(jnp.float32) * total[:levels]
@@ -335,7 +329,16 @@
     def finish_after(j, relays, lasts):
         if j >= extra:
             arrive(j + 1, due_mid)
-            arrive(j + SPAN - 2 * own + 1, relays)
+            reached = j + SPAN - 2 * own
+            arrive(reached + 1, relays)
+            spread[:, cols(j, j + 1)] += from_above(
+                j, 1, 2 * own + reached - reached % 2, 2 * own + reached + 1
+            )
+            if reached % 2 == 1:
+                for later in range(j + 1, own):
+                    spread[:, cols(later, later + 1)] += from_above(
+                        later, 1, 2 * own + reached - 1, 2 * own + reached + 1
+                    )
         else:
             arrive(j + 1, lasts)
         finish(j)

time: 32.6 us -> 32.3 us (level)
  Pallas kernels: 31.8 us -> 31.4 us
    pallas_call x1, Pallas kernels: 31.8 us -> 31.4 us  [per_device(): pl.pallas_call(functools.partial(kernel, sizes), out_shape=jax.ShapeDtype...]
where the time goes in v6:
time: 32.3 us; the launch traced here: 32.1 us
  Pallas kernels  31.4 us (97%)
  local copies, waits for them, and re-layouts  0.71 us (2%)
    pallas_call x1, Pallas kernels, per_device(): pl.pallas_call(functools.partial(kernel, sizes), out_shape=jax.ShapeDtype...  31.4 us
    unnamed x1, local copies, waits for them, and re-layouts  0.71 us

profile of v6, /device:TPU:26, one launch (start us, length us, event | category | flops | bytes accessed | tf_op | source)
XLA Modules:
  0.0 32.1 jit_solution(6970337332340373946)
XLA Ops:
  0.0 31.4 %shard_map.64 = f32[4,32,512]{2,1,0:T(8,128)S(1)} custom-call(s32[8]{0:T(128)} %count_hbm.1, s32[32]{0:T(128)} %level_hbm.1, s32[2,96]{1,0:T(2,128)} %bitcast.1, bf16[10,4,32,1024]{3,2,1,0:T(8,128)(2,1)} %ens_hbm.1, f32[4,32,1024]{2,1,0:T(8,128)} %control_hbm.1, bf16[96,128,128]{2,1,0:T(8,128)(2,1)} %loc_hbm.1), custom_call_target="tpu_custom_call" | custom-call | flops 2013265920 | bytes 6291456 | tf_op jit(solution)/shard_map/pallas_call | solution.py:397
  31.4 0.7 %copy.8 = f32[4,32,512]{2,1,0:T(8,128)} copy(f32[4,32,512]{2,1,0:T(8,128)S(1)} %shard_map.64) | data formatting | bytes 524288

commit v7 on v6

--- a/solution.py
+++ b/solution.py
@@ -15,7 +15,8 @@
 
 
 def pieces_of(own):
-    return [(first, 2) for first in range(0, own, 2)]
+    extra = SPAN - own
+    return [(first, 2) for first in (*range(own - extra, own, 2), *range(0, own - extra, 2))]
 
 
 def messages_of(count):
@@ -87,7 +88,7 @@
         )
     for copy in small:
         copy.start()
-    for first, n in pieces[:2]:
+    for first, n in pieces[: extra // 2]:
         for copy in loads[first]:
             copy.start()
 
@@ -223,16 +224,19 @@
                     table.dtype
                 )
 
-    for first, n in pieces:
+    def lift_and_send(first, n):
         lift(first, n)
-        if first == 0:
-            for later, unused in pieces[2:]:
+        if first == pieces[0][0]:
+            load_pairs.start()
+            load_loc.start()
+            for later, unused in pieces[extra // 2 :]:
                 for copy in loads[later]:
                     copy.start()
-            load_pairs.start()
-            load_loc.start()
             pl.semaphore_wait(barrier, 2 + peers - 1)
         lift_own[first].start()
+
+    for first, n in pieces[: extra // 2]:
+        lift_and_send(first, n)
 
     load_pairs.wait()
     low = 7
@@ -262,14 +266,24 @@
         j = 2 * own + n
         keep_far(own + n, from_below(j, 2, j - SPAN, own))
     far_two.start()
+
+    for first, n in pieces[extra // 2 :]:
+        lift_and_send(first, n)
+
     for n in range(extra, own, 2):
         j = own + n
         keep_far(n, from_below(j, 2, j - SPAN, own))
         far_mid[n].start()
 
-    for first, n in messages_of(extra):
-        arrive(first + n)
-        lift_relay[first].start()
+    first_core = lax.rem(here, 2) == 0
+
+    def relay():
+        waiting = dict(due)
+        for first, n in messages_of(extra):
+            arrive(first + n, waiting)
+            lift_relay[first].start()
+
+    pl.when(first_core)(relay)
 
     for n in range(0, extra, 2):
         j = own + n
@@ -284,6 +298,10 @@
 
     for j in range(0, own, 2):
         spread[:, cols(j, j + 2)] = from_above(j, 2, j, own) + from_below(j, 2, 0, j + 1)
+
+    pl.when(jnp.logical_not(first_core))(relay)
+    for first in [f for f in due if f < extra]:
+        due.pop(first)
 
     for first in range(0, own, 2):
         arrive(first + 2)
@@ -345,7 +363,6 @@
 
     for j in order[:-2]:
         finish_after(j, due_relay, due_far)
-    first_core = lax.rem(here, 2) == 0
     for turn, chosen in ((order[-2:], first_core), (order[:-3:-1], jnp.logical_not(first_core))):
 
         @pl.when(chosen)

time: 32.3 us -> 32.6 us (level)
  the two profiles are of different devices: /device:TPU:26 before, /device:TPU:1 now
where the time goes in v7:
time: 32.6 us; the launch traced here: 32.5 us
  Pallas kernels  31.8 us (98%)
  local copies, waits for them, and re-layouts  0.71 us (2%)
    pallas_call x1, Pallas kernels, per_device(): pl.pallas_call(functools.partial(kernel, sizes), out_shape=jax.ShapeDtype...  31.8 us
    unnamed x1, local copies, waits for them, and re-layouts  0.71 us

profile of v7, /device:TPU:1, one launch (start us, length us, event | category | flops | bytes accessed | tf_op | source)
XLA Modules:
  0.0 32.5 jit_solution(14034784731839809079)
XLA Ops:
  0.0 31.8 %shard_map.64 = f32[4,32,512]{2,1,0:T(8,128)S(1)} custom-call(s32[8]{0:T(128)} %count_hbm.1, s32[32]{0:T(128)} %level_hbm.1, s32[2,96]{1,0:T(2,128)} %bitcast.1, bf16[10,4,32,1024]{3,2,1,0:T(8,128)(2,1)} %ens_hbm.1, f32[4,32,1024]{2,1,0:T(8,128)} %control_hbm.1, bf16[96,128,128]{2,1,0:T(8,128)(2,1)} %loc_hbm.1), custom_call_target="tpu_custom_call" | custom-call | flops 2013265920 | bytes 6291456 | tf_op jit(solution)/shard_map/pallas_call | solution.py:414
  31.8 0.7 %copy.8 = f32[4,32,512]{2,1,0:T(8,128)} copy(f32[4,32,512]{2,1,0:T(8,128)S(1)} %shard_map.64) | data formatting | bytes 524288
